TPU v7x, 256 devices: a whole 4x4x8 slice. The times are simulated.
256 devices in a mesh: cgrp: 8 (over z), dev: 32 (over x, y, core).
Axes of the slice: x: 4, y: 4, z: 8, core: 2. Of those that a mesh axis runs over, the one named last changes fastest.
Arguments:
- docs: bfloat16 [65536, 1024], P('dev'), may hold values from -140 to 140
- centroids: float32 [8192, 1024], P(('cgrp', 'dev')), may hold values from -6 to 6
Outputs:
- centroids_next: float32 [8192, 1024], P(('cgrp', 'dev'))
- mass: float32 [8192], P(('cgrp', 'dev'))
- doc_lse: float32 [65536], P('dev')
All inputs are finite; a program needn't handle non-finite values.
Results may differ from a plain program's by a relative error of at most 0.012.
The roundings to bfloat16 on the way count: a program that leaves them out, or rounds other values in their place, can miss the bound.
Values may be sent and summed in bfloat16 or wider, within the bound.
A program may use at most 64 MiB of HBM per device.

v0:
```python
import math
import jax
import jax.numpy as jnp
from jax import lax
from jax.sharding import PartitionSpec as P


def body(docs, centroids):
    width = docs.shape[1]
    scale = 4.0 / math.sqrt(width)
    rounded = centroids.astype(jnp.bfloat16)
    gathered = lax.all_gather(rounded, "dev", axis=0, tiled=True)
    gathered_wide = gathered.astype(jnp.float32)
    gathered_norms = jnp.sum(gathered_wide * gathered_wide, axis=1)
    dots = lax.dot_general(
        docs, gathered, (((1,), (1,)), ((), ())), preferred_element_type=jnp.float32
    )
    scores = (dots - 0.5 * gathered_norms[None, :]) * scale
    local_max = jnp.max(scores, axis=1)
    local_sum = jnp.sum(jnp.exp(scores - local_max[:, None]), axis=1)
    group_top = lax.pmax(local_max, "cgrp")
    group_sum = lax.psum(local_sum * jnp.exp(local_max - group_top), "cgrp")
    doc_lse = group_top + jnp.log(group_sum)
    resp = jnp.exp(scores - doc_lse[:, None])
    docs_wide = docs.astype(jnp.float32)
    local_mass = jnp.sum(resp, axis=0)
    term = lax.dot_general(
        resp,
        docs_wide,
        (((0,), (0,)), ((), ())),
        preferred_element_type=jnp.float32,
        precision=lax.Precision.HIGHEST,
    )
    weighted, mass = (
        lax.psum_scatter(term, "dev", scatter_dimension=0, tiled=True),
        lax.psum_scatter(local_mass, "dev", scatter_dimension=0, tiled=True),
    )
    centroids_next = (weighted + centroids) / (mass[:, None] + 1.0)
    return (centroids_next, mass, doc_lse)


def solution(mesh):
    in_specs = (P("dev", None), P(("cgrp", "dev"), None))
    out_specs = (P(("cgrp", "dev"), None), P(("cgrp", "dev")), P("dev"))
    return jax.shard_map(body, mesh=mesh, in_specs=in_specs, out_specs=out_specs, check_vma=False)
```

profile of v0, /device:TPU:2, one launch (start us, length us, event | category | flops | bytes accessed | tf_op | source)
XLA Modules:
  0.0 227.5 jit_solution(16202654459003388817)
XLA Ops:
  7.2 0.0 all-gather.2.cloned.1.call-start
  7.2 1.5 convert_element_type.7
  8.8 0.0 all-gather.2.cloned.1.call-update
  8.8 0.0 reduce-scatter.2.cloned.1.call-start
  8.8 53.7 %all-gather.2.cloned.1.call-done = bf16[1024,1024]{1,0:T(8,128)(2,1)} async-done(((bf16[32,1024]{1,0:T(8,128)(2,1)}), bf16[1024,1024]{1,0:T(8,128)(2,1)}) %all-gather.2.cloned.1.call-update) | async-done | bytes 2097168 | tf_op jit(solution)/shard_map/all_gather | solution.py:12
  62.5 2.1 multiply_reduce_fusion
  64.6 10.6 %fusion.2 = (f32[2048]{0:T(1024)S(1)}, f32[2048,1024]{0,1:T(8,128)}) fusion(f32[1024]{0:T(1024)S(1)} %broadcast_multiply_fusion, bf16[2048,1024]{1,0:T(8,128)(2,1)} %param.2, bf16[1024,1024]{1,0:T(8,128)(2,1)} %all-gather.2.cloned.1.call-done), kind=kOutput, calls=%fused_computation.5 | convolution fusion | flops 4301256704 | bytes 14692352 | tf_op jit(solution)/shard_map/dot_general | solution.py:15
  75.2 17.7 %pmax.7 = f32[2048]{0:T(1024)S(1)} all-reduce(f32[2048]{0:T(1024)S(1)} %get-tuple-element.5), channel_id=1, replica_groups=mesh['cgrp'=8,'dev'=32] {'cgrp'}, use_global_device_ids=true, to_apply=%region_2.0 | all-reduce | flops 2048 | bytes 16384 | tf_op jit(solution)/shard_map/pmax | solution.py:21
  92.9 4.5 %exponential_reduce_fusion = f32[2048]{0:T(1024)S(1)} fusion(f32[2048,1024]{0,1:T(8,128)} %get-tuple-element.6, f32[2048]{0:T(1024)S(1)} %get-tuple-element.5, f32[1024]{0:T(1024)S(1)} %broadcast_multiply_fusion), kind=kLoop, calls=%fused_computation.1 | loop fusion | flops 8386560 | bytes 8409088 | tf_op jit(solution)/shard_map/reduce_sum | solution.py:20
  97.4 15.5 %psum.7 = f32[2048]{0:T(1024)S(1)} all-reduce(f32[2048]{0:T(1024)S(1)} %exponential_multiply_fusion), channel_id=1, replica_groups=mesh['cgrp'=8,'dev'=32] {'cgrp'}, use_global_device_ids=true, to_apply=%region_4.0 | all-reduce | flops 2048 | bytes 16384 | tf_op jit(solution)/shard_map/psum | solution.py:22
  112.9 0.0 copy-start.1
  112.9 0.0 copy-start.2
  113.0 19.1 %fusion.1 = f32[1024,1024]{1,0:T(8,128)} fusion(bf16[2048,1024]{1,0:T(8,128)(2,1)} %param.2, f32[2048,1024]{0,1:T(8,128)} %get-tuple-element.6, f32[2048]{0:T(1024)S(1)} %log_add_fusion, f32[1024]{0:T(1024)S(1)} %broadcast_multiply_fusion), kind=kOutput, calls=%fused_computation.4 | convolution fusion | flops 25776095232 | bytes 16789504 | tf_op jit(solution)/shard_map/dot_general | solution.py:27
  132.1 0.0 copy-start
  132.1 0.0 reduce-scatter.2.cloned.1.call-update
  132.1 0.0 copy-done.2
  132.1 0.6 dynamic-slice
  133.3 0.0 copy-done.1
  133.4 4.5 %fusion = f32[1024]{0:T(1024)S(1)} fusion(f32[2048,1024]{0,1:T(8,128)} %get-tuple-element.6, f32[2048]{0:T(1024)S(1)} %log_add_fusion, f32[1024]{0:T(1024)S(1)} %broadcast_multiply_fusion), kind=kLoop, calls=%fused_computation.3 | loop fusion | flops 8387584 | bytes 8404992 | tf_op jit(solution)/shard_map/reduce_sum | solution.py:26
  137.9 53.2 %all-reduce = f32[1024]{0:T(1024)S(1)} all-reduce(f32[1024]{0:T(1024)S(1)} %fusion), channel_id=3, replica_groups=mesh['cgrp'=8,'dev'=32] {'dev'}, use_global_device_ids=true, to_apply=%region_7.0.clone | all-reduce | flops 1024 | bytes 8192
  191.0 0.6 broadcast_add_fusion
  191.6 27.5 %reduce-scatter.2.cloned.1.call-done = f32[32,1024]{1,0:T(8,128)} async-done(((f32[1024,1024]{1,0:T(8,128)}), f32[32,1024]{1,0:T(8,128)}) %reduce-scatter.2.cloned.1.call-update) | async-done | bytes 131088 | tf_op jit(solution)/shard_map/reduce_scatter | solution.py:35
  219.1 0.0 copy-done
  219.1 1.6 add_divide_fusion
  (3 shorter events, 0.0 us)
Async XLA Ops:
  7.2 55.4 %all-gather.2.cloned.1.call-start = ((), (), s32[]{:S(2)}) async-start(), calls=%async_computation.1 | async-start | bytes 2162688 | tf_op jit(solution)/shard_map/all_gather | solution.py:12
  8.8 210.3 %reduce-scatter.2.cloned.1.call-start = ((), (), s32[]{:S(2)}) async-start(), calls=%async_computation.2 | async-start | bytes 4325376 | tf_op jit(solution)/shard_map/reduce_scatter | solution.py:35
  112.9 20.4 %copy-start.1 = (f32[2048]{0:T(1024)}, f32[2048]{0:T(1024)S(1)}, u32[]{:S(2)}) copy-start(f32[2048]{0:T(1024)S(1)} %log_add_fusion) | copy-start | bytes 24580
  112.9 19.2 %copy-start.2 = (u32[256]{0:T(256)S(1)}, u32[256]{0:T(256)}, u32[]{:S(2)}) copy-start(u32[256]{0:T(256)} %constant.13) | copy-start | bytes 3076
  132.1 87.0 %copy-start = (f32[32,1024]{1,0:T(8,128)S(1)}, f32[32,1024]{1,0:T(8,128)}, u32[]{:S(2)}) copy-start(f32[32,1024]{1,0:T(8,128)} %param.3) | copy-start | bytes 393220
Sparse Core Ops, SparseCore 0:
  11.1 51.3 all-gather.1
  132.2 86.8 reduce-scatter.1
where the time goes:
time: 228 us
  blocking collectives  86.3 us (38%)
  waiting for transfers between devices  81.2 us (36%)
  matrix products  29.7 us (13%)
  other arithmetic  14.9 us (7%)
  between operations  14.8 us (6%)
    all_gather x1, waiting for transfers between devices, body(): gathered = lax.all_gather(rounded, 'dev', axis=0, tiled=True)  53.7 us
    unnamed x1, blocking collectives  53.2 us
    reduce_scatter x1, waiting for transfers between devices, body(): lax.psum_scatter(term, 'dev', scatter_dimension=0, tiled=True)  27.5 us
    dot_general x1, matrix products, body(): lax.dot_general(resp, docs_wide, (((0,), (0,)), ((), ())), preferred_elem...  19.1 us
    pmax x1, blocking collectives, body(): group_top = lax.pmax(local_max, 'cgrp')  17.7 us
    psum x1, blocking collectives, body(): group_sum = lax.psum(local_sum * jnp.exp(local_max - group_top), 'cgrp')  15.5 us
    dot_general x1, matrix products, body(): lax.dot_general(docs, gathered, (((1,), (1,)), ((), ())), preferred_eleme...  10.6 us
  transfers between devices with their start and end apart: 2, of which 2 were waited for; matrix products, arithmetic and copies ran while one was open for 2% of the time, Pallas kernels for 0%

commit v1 on v0

--- a/solution.py
+++ b/solution.py
@@ -9,7 +9,9 @@
     width = docs.shape[1]
     scale = 4.0 / math.sqrt(width)
     rounded = centroids.astype(jnp.bfloat16)
-    gathered = lax.all_gather(rounded, "dev", axis=0, tiled=True)
+    gathered = jnp.concatenate(
+        lax.all_to_all(jnp.stack([rounded] * lax.axis_size("dev")), "dev", 0, 0), axis=0
+    )
     gathered_wide = gathered.astype(jnp.float32)
     gathered_norms = jnp.sum(gathered_wide * gathered_wide, axis=1)
     dots = lax.dot_general(

time: 228 us -> 205 us (0.90)
  waiting for transfers between devices: 81.2 us -> 27.8 us
  blocking collectives: 86.3 us -> 121 us
    all_gather x1 -> x0, waiting for transfers between devices: 53.7 us -> none  [body(): gathered = lax.all_gather(rounded, 'dev', axis=0, tiled=True)]
    all_to_all x0 -> x1, blocking collectives: none -> 33.1 us  [body(): lax.all_to_all(jnp.stack([rounded] * lax.axis_size('dev')), 'dev', 0, 0)]
    pmax x1, blocking collectives: 17.7 us -> 20.3 us  [body(): group_top = lax.pmax(local_max, 'cgrp')]
  transfers between devices with their start and end apart: 2 -> 1, of which waited for: 2 -> 1; matrix products, arithmetic and copies ran while one was open for 2% -> 3% of each run, Pallas kernels for 0% -> 0%
where the time goes in v1:
time: 205 us
  blocking collectives  121 us (59%)
  matrix products  28 us (14%)
  waiting for transfers between devices  27.8 us (14%)
  between operations  14.8 us (7%)
  other arithmetic  12.7 us (6%)
    unnamed x1, blocking collectives  53.1 us
    all_to_all x1, blocking collectives, body(): lax.all_to_all(jnp.stack([rounded] * lax.axis_size('dev')), 'dev', 0, 0)  33.1 us
    reduce_scatter x1, waiting for transfers between devices, body(): lax.psum_scatter(term, 'dev', scatter_dimension=0, tiled=True)  27.8 us
    pmax x1, blocking collectives, body(): group_top = lax.pmax(local_max, 'cgrp')  20.3 us
    dot_general x1, matrix products, body(): lax.dot_general(resp, docs_wide, (((0,), (0,)), ((), ())), preferred_elem...  19.1 us
    psum x1, blocking collectives, body(): group_sum = lax.psum(local_sum * jnp.exp(local_max - group_top), 'cgrp')  14.4 us
    dot_general x1, matrix products, body(): lax.dot_general(docs, gathered, (((1,), (1,)), ((), ())), preferred_eleme...  8.94 us
    reduce_sum x1, other arithmetic, body(): local_sum = jnp.sum(jnp.exp(scores - local_max[:, None]), axis=1)  4.51 us
  transfers between devices with their start and end apart: 1, of which 1 were waited for; matrix products, arithmetic and copies ran while one was open for 3% of the time, Pallas kernels for 0%

profile of v1, /device:TPU:2, one launch (start us, length us, event | category | flops | bytes accessed | tf_op | source)
XLA Modules:
  0.0 205.2 jit_solution(16600731884991146847)
XLA Ops:
  7.2 0.0 reduce-scatter.2.cloned.1.call-start
  7.2 0.9 convert_element_type.8
  8.1 0.2 stack.2
  8.4 33.1 %all_to_all.5 = bf16[32,32,1024]{2,1,0:T(8,128)(2,1)S(1)} all-to-all(bf16[32,32,1024]{2,1,0:T(8,128)(2,1)S(1)} %stack.2), channel_id=1, replica_groups=mesh['cgrp'=8,'dev'=32] {'dev'}, dimensions={0} | all-to-all | bytes 4194304 | tf_op jit(solution)/shard_map/all_to_all | solution.py:13
  41.5 0.5 multiply_reduce_fusion
  42.0 0.1 mul.30
  42.0 8.9 %fusion.2 = (f32[2048]{0:T(1024)S(1)}, f32[2048,1024]{0,1:T(8,128)}) fusion(f32[1024]{0:T(1024)S(1)} %mul.30, bf16[2048,1024]{1,0:T(8,128)(2,1)} %param.2, bf16[1024,1024]{1,0:T(8,128)(2,1)S(1)} %bitcast.5), kind=kOutput, calls=%fused_computation.5 | convolution fusion | flops 4301256704 | bytes 14692352 | tf_op jit(solution)/shard_map/dot_general | solution.py:17
  51.0 20.3 %pmax.7 = f32[2048]{0:T(1024)S(1)} all-reduce(f32[2048]{0:T(1024)S(1)} %get-tuple-element.5), channel_id=1, replica_groups=mesh['cgrp'=8,'dev'=32] {'cgrp'}, use_global_device_ids=true, to_apply=%region_2.0 | all-reduce | flops 2048 | bytes 16384 | tf_op jit(solution)/shard_map/pmax | solution.py:23
  71.2 4.5 %exponential_reduce_fusion = f32[2048]{0:T(1024)S(1)} fusion(f32[2048,1024]{0,1:T(8,128)} %get-tuple-element.6, f32[2048]{0:T(1024)S(1)} %get-tuple-element.5, f32[1024]{0:T(1024)S(1)} %mul.30), kind=kLoop, calls=%fused_computation.1 | loop fusion | flops 8386560 | bytes 8409088 | tf_op jit(solution)/shard_map/reduce_sum | solution.py:22
  75.8 14.4 %psum.7 = f32[2048]{0:T(1024)S(1)} all-reduce(f32[2048]{0:T(1024)S(1)} %exponential_multiply_fusion), channel_id=1, replica_groups=mesh['cgrp'=8,'dev'=32] {'cgrp'}, use_global_device_ids=true, to_apply=%region_4.0 | all-reduce | flops 2048 | bytes 16384 | tf_op jit(solution)/shard_map/psum | solution.py:24
  90.2 0.0 copy-start.1
  90.2 0.0 copy-start.2
  90.2 19.1 %fusion.1 = f32[1024,1024]{1,0:T(8,128)} fusion(bf16[2048,1024]{1,0:T(8,128)(2,1)} %param.2, f32[2048,1024]{0,1:T(8,128)} %get-tuple-element.6, f32[2048]{0:T(1024)S(1)} %log_add_fusion, f32[1024]{0:T(1024)S(1)} %mul.30), kind=kOutput, calls=%fused_computation.4 | convolution fusion | flops 25776095232 | bytes 16789504 | tf_op jit(solution)/shard_map/dot_general | solution.py:29
  109.3 0.0 copy-start
  109.3 0.0 reduce-scatter.2.cloned.1.call-update
  109.4 0.0 copy-done.2
  109.4 0.6 dynamic-slice
  110.6 0.0 copy-done.1
  110.6 4.5 %fusion = f32[1024]{0:T(1024)S(1)} fusion(f32[2048,1024]{0,1:T(8,128)} %get-tuple-element.6, f32[2048]{0:T(1024)S(1)} %log_add_fusion, f32[1024]{0:T(1024)S(1)} %mul.30), kind=kLoop, calls=%fused_computation.3 | loop fusion | flops 8387584 | bytes 8404992 | tf_op jit(solution)/shard_map/reduce_sum | solution.py:28
  115.1 53.1 %all-reduce = f32[1024]{0:T(1024)S(1)} all-reduce(f32[1024]{0:T(1024)S(1)} %fusion), channel_id=3, replica_groups=mesh['cgrp'=8,'dev'=32] {'dev'}, use_global_device_ids=true, to_apply=%region_7.0.clone | all-reduce | flops 1024 | bytes 8192
  168.3 0.6 broadcast_add_fusion
  168.9 27.8 %reduce-scatter.2.cloned.1.call-done = f32[32,1024]{1,0:T(8,128)} async-done(((f32[1024,1024]{1,0:T(8,128)}), f32[32,1024]{1,0:T(8,128)}) %reduce-scatter.2.cloned.1.call-update) | async-done | bytes 131088 | tf_op jit(solution)/shard_map/reduce_scatter | solution.py:37
  196.7 0.0 copy-done
  196.7 1.6 add_divide_fusion
  (3 shorter events, 0.0 us)
Async XLA Ops:
  7.2 189.5 %reduce-scatter.2.cloned.1.call-start = ((), (), s32[]{:S(2)}) async-start(), calls=%async_computation.2 | async-start | bytes 4325376 | tf_op jit(solution)/shard_map/reduce_scatter | solution.py:37
  90.2 20.4 %copy-start.1 = (f32[2048]{0:T(1024)}, f32[2048]{0:T(1024)S(1)}, u32[]{:S(2)}) copy-start(f32[2048]{0:T(1024)S(1)} %log_add_fusion) | copy-start | bytes 24580
  90.2 19.2 %copy-start.2 = (u32[256]{0:T(256)S(1)}, u32[256]{0:T(256)}, u32[]{:S(2)}) copy-start(u32[256]{0:T(256)} %constant.13) | copy-start | bytes 3076
  109.3 87.3 %copy-start = (f32[32,1024]{1,0:T(8,128)S(1)}, f32[32,1024]{1,0:T(8,128)}, u32[]{:S(2)}) copy-start(f32[32,1024]{1,0:T(8,128)} %param.3) | copy-start | bytes 393220
Sparse Core Ops, SparseCore 0:
  109.5 87.1 reduce-scatter.1

commit v2 on v0

--- a/solution.py
+++ b/solution.py
@@ -19,7 +19,7 @@
     local_max = jnp.max(scores, axis=1)
     local_sum = jnp.sum(jnp.exp(scores - local_max[:, None]), axis=1)
     group_top = lax.pmax(local_max, "cgrp")
-    group_sum = lax.psum(local_sum * jnp.exp(local_max - group_top), "cgrp")
+    group_sum = jnp.sum(lax.all_gather(local_sum * jnp.exp(local_max - group_top), "cgrp"), axis=0)
     doc_lse = group_top + jnp.log(group_sum)
     resp = jnp.exp(scores - doc_lse[:, None])
     docs_wide = docs.astype(jnp.float32)

time: 228 us -> 237 us (1.039)
  blocking collectives: 86.3 us -> 95.7 us
    all_gather x0 -> x1, blocking collectives: none -> 24.7 us  [body(): lax.all_gather(local_sum * jnp.exp(local_max - group_top), 'cgrp')]
    psum x1 -> x0, blocking collectives: 15.5 us -> none  [body(): group_sum = lax.psum(local_sum * jnp.exp(local_max - group_top), 'cgrp')]
where the time goes in v2:
time: 237 us; the launch traced here: 236 us
  blocking collectives  95.7 us (40%)
  waiting for transfers between devices  80.6 us (34%)
  matrix products  29.7 us (13%)
  other arithmetic  14.9 us (6%)
  between operations  14.8 us (6%)
    all_gather x1, waiting for transfers between devices, body(): gathered = lax.all_gather(rounded, 'dev', axis=0, tiled=True)  53.7 us
    unnamed x1, blocking collectives  53.2 us
    reduce_scatter x1, waiting for transfers between devices, body(): lax.psum_scatter(term, 'dev', scatter_dimension=0, tiled=True)  26.9 us
    all_gather x1, blocking collectives, body(): lax.all_gather(local_sum * jnp.exp(local_max - group_top), 'cgrp')  24.7 us
    dot_general x1, matrix products, body(): lax.dot_general(resp, docs_wide, (((0,), (0,)), ((), ())), preferred_elem...  19.1 us
    pmax x1, blocking collectives, body(): group_top = lax.pmax(local_max, 'cgrp')  17.7 us
    dot_general x1, matrix products, body(): lax.dot_general(docs, gathered, (((1,), (1,)), ((), ())), preferred_eleme...  10.6 us
  transfers between devices with their start and end apart: 2, of which 2 were waited for; matrix products, arithmetic and copies ran while one was open for 2% of the time, Pallas kernels for 0%

profile of v2, /device:TPU:2, one launch (start us, length us, event | category | flops | bytes accessed | tf_op | source)
XLA Modules:
  0.0 236.4 jit_solution(15914247017447422261)
XLA Ops:
  7.2 0.0 all-gather.3.cloned.1.call-start
  7.2 1.5 convert_element_type.7
  8.8 0.0 all-gather.3.cloned.1.call-update
  8.8 0.0 reduce-scatter.2.cloned.1.call-start
  8.8 53.7 %all-gather.3.cloned.1.call-done = bf16[1024,1024]{1,0:T(8,128)(2,1)} async-done(((bf16[32,1024]{1,0:T(8,128)(2,1)}), bf16[1024,1024]{1,0:T(8,128)(2,1)}) %all-gather.3.cloned.1.call-update) | async-done | bytes 2097168 | tf_op jit(solution)/shard_map/all_gather | solution.py:12
  62.5 2.1 multiply_reduce_fusion
  64.6 10.6 %fusion.2 = (f32[2048]{0:T(1024)S(1)}, f32[2048,1024]{0,1:T(8,128)}) fusion(f32[1024]{0:T(1024)S(1)} %broadcast_multiply_fusion, bf16[2048,1024]{1,0:T(8,128)(2,1)} %param.2, bf16[1024,1024]{1,0:T(8,128)(2,1)} %all-gather.3.cloned.1.call-done), kind=kOutput, calls=%fused_computation.5 | convolution fusion | flops 4301256704 | bytes 14692352 | tf_op jit(solution)/shard_map/dot_general | solution.py:15
  75.2 17.7 %pmax.7 = f32[2048]{0:T(1024)S(1)} all-reduce(f32[2048]{0:T(1024)S(1)} %get-tuple-element.5), channel_id=1, replica_groups=mesh['cgrp'=8,'dev'=32] {'cgrp'}, use_global_device_ids=true, to_apply=%region_2.0 | all-reduce | flops 2048 | bytes 16384 | tf_op jit(solution)/shard_map/pmax | solution.py:21
  92.9 4.5 %exponential_reduce_fusion = f32[2048]{0:T(1024)S(1)} fusion(f32[2048,1024]{0,1:T(8,128)} %get-tuple-element.6, f32[2048]{0:T(1024)S(1)} %get-tuple-element.5, f32[1024]{0:T(1024)S(1)} %broadcast_multiply_fusion), kind=kLoop, calls=%fused_computation.1 | loop fusion | flops 8386560 | bytes 8409088 | tf_op jit(solution)/shard_map/reduce_sum | solution.py:20
  97.4 24.7 %all-gather = f32[16384]{0:T(1024)S(1)} all-gather(f32[2048]{0:T(1024)S(1)} %exponential_multiply_fusion), channel_id=2, replica_groups=mesh['cgrp'=8,'dev'=32] {'cgrp'}, dimensions={0}, use_global_device_ids=true | all-gather | bytes 73728 | tf_op jit(solution)/shard_map/all_gather | solution.py:22
  122.2 0.0 copy-start.1
  122.3 0.0 copy-start.2
  122.3 19.1 %fusion.1 = f32[1024,1024]{1,0:T(8,128)} fusion(bf16[2048,1024]{1,0:T(8,128)(2,1)} %param.2, f32[2048,1024]{0,1:T(8,128)} %get-tuple-element.6, f32[2048]{0:T(1024)S(1)} %log_add_fusion, f32[1024]{0:T(1024)S(1)} %broadcast_multiply_fusion), kind=kOutput, calls=%fused_computation.4 | convolution fusion | flops 25776095232 | bytes 16789504 | tf_op jit(solution)/shard_map/dot_general | solution.py:27
  141.4 0.0 copy-start
  141.4 0.0 reduce-scatter.2.cloned.1.call-update
  141.4 0.0 copy-done.2
  141.4 0.6 dynamic-slice
  142.7 0.0 copy-done.1
  142.7 4.5 %fusion = f32[1024]{0:T(1024)S(1)} fusion(f32[2048,1024]{0,1:T(8,128)} %get-tuple-element.6, f32[2048]{0:T(1024)S(1)} %log_add_fusion, f32[1024]{0:T(1024)S(1)} %broadcast_multiply_fusion), kind=kLoop, calls=%fused_computation.3 | loop fusion | flops 8387584 | bytes 8404992 | tf_op jit(solution)/shard_map/reduce_sum | solution.py:26
  147.2 53.2 %all-reduce = f32[1024]{0:T(1024)S(1)} all-reduce(f32[1024]{0:T(1024)S(1)} %fusion), channel_id=4, replica_groups=mesh['cgrp'=8,'dev'=32] {'dev'}, use_global_device_ids=true, to_apply=%region_7.0.clone | all-reduce | flops 1024 | bytes 8192
  200.4 0.6 broadcast_add_fusion
  201.0 26.9 %reduce-scatter.2.cloned.1.call-done = f32[32,1024]{1,0:T(8,128)} async-done(((f32[1024,1024]{1,0:T(8,128)}), f32[32,1024]{1,0:T(8,128)}) %reduce-scatter.2.cloned.1.call-update) | async-done | bytes 131088 | tf_op jit(solution)/shard_map/reduce_scatter | solution.py:35
  227.9 0.0 copy-done
  227.9 1.6 add_divide_fusion
  (5 shorter events, 0.1 us)
Async XLA Ops:
  7.2 55.4 %all-gather.3.cloned.1.call-start = ((), (), s32[]{:S(2)}) async-start(), calls=%async_computation.1 | async-start | bytes 2162688 | tf_op jit(solution)/shard_map/all_gather | solution.py:12
  8.8 219.1 %reduce-scatter.2.cloned.1.call-start = ((), (), s32[]{:S(2)}) async-start(), calls=%async_computation.2 | async-start | bytes 4325376 | tf_op jit(solution)/shard_map/reduce_scatter | solution.py:35
  122.2 20.4 %copy-start.1 = (f32[2048]{0:T(1024)}, f32[2048]{0:T(1024)S(1)}, u32[]{:S(2)}) copy-start(f32[2048]{0:T(1024)S(1)} %log_add_fusion) | copy-start | bytes 24580
  122.3 19.2 %copy-start.2 = (u32[256]{0:T(256)S(1)}, u32[256]{0:T(256)}, u32[]{:S(2)}) copy-start(u32[256]{0:T(256)} %constant.13) | copy-start | bytes 3076
  141.4 86.5 %copy-start = (f32[32,1024]{1,0:T(8,128)S(1)}, f32[32,1024]{1,0:T(8,128)}, u32[]{:S(2)}) copy-start(f32[32,1024]{1,0:T(8,128)} %param.3) | copy-start | bytes 393220
Sparse Core Ops, SparseCore 0:
  11.1 51.3 all-gather.2
  141.5 86.3 reduce-scatter.1
